TPU v7x, 32 devices: a whole 2x2x4 slice. The times are simulated.
32 devices in a mesh: gx: 4 (over y, x), gy: 8 (over z, core).
Axes of the slice: x: 2, y: 2, z: 4, core: 2. Of those that a mesh axis runs over, the one named last changes fastest.
Arguments:
- old_state: float32 [256, 6, 32768], P(('gx', 'gy')), may hold values from -6 to 6
- old_owner: int32 [128], replicated, may hold values from 0 to 31, as said below
- old_slot: int32 [128], replicated, may hold values from 0 to 7, as said below
- diffusivity: float32 [6], replicated, may hold values from 0.01 to 0.08
Outputs:
- new_state: float32 [128, 6, 32768], P(('gx', 'gy'))
Inputs may be any that keep to these rules, and one draw needn't show every extreme that they name: The curve is closed: with n = g // 4 the new owner of box g, old_owner[g] is n, or n - 1 modulo the device count for one of the first 2 boxes of n, or n + 1 modulo the device count for one of the last 2 boxes of n. `old_slot`: A box kept by its owner sits in slot 2 + g % 4; the j-th of the first 2 boxes of a device, when held by the device below, sat in that device's slot 6 + j; the j-th of the last 2 boxes, when held by the device above, sat in its slot j. Slots that hold no box hold anything. Some device takes over 2 boxes from each neighbour in every draw.
All inputs are finite; a program needn't handle non-finite values.
Results may differ from a plain program's by a relative error of at most 0.0003.
Values sent between devices are 32-bit elements; how exact they have to be, the bound alone decides.
A program may use at most 128 MiB of HBM per device.

v0:
```python
import jax
import jax.numpy as jnp
from jax import lax
from jax.sharding import PartitionSpec as P

B = 32
F = 6
CAP = 4
DRIFT = 2


courant = 0.25


def shifted(block, axis, distance):
    devices = range(lax.axis_size(axis))
    route = [((i - distance) % len(devices), i) for i in devices]
    return lax.ppermute(block, axis, route)


def padded_2(block, sides, width):
    for axis, dim in sides:
        count = lax.axis_size(axis)
        forward = [(i, i + 1) for i in range(count - 1)]
        backward = [(target, source) for source, target in forward]
        low = lax.ppermute(
            lax.slice_in_dim(block, block.shape[dim] - width, None, axis=dim), axis, forward
        )
        high = lax.ppermute(lax.slice_in_dim(block, 0, width, axis=dim), axis, backward)
        block = jnp.concatenate([low, block, high], axis=dim)
    return block


def minmod(former, latter):
    return (
        0.5 * (jnp.sign(former) + jnp.sign(latter)) * jnp.minimum(jnp.abs(former), jnp.abs(latter))
    )


def part_of(values, bottom, ceiling, dimension):
    return lax.slice_in_dim(values, bottom, ceiling, axis=dimension)


def along(stripe, dimension, velocity_index, spread):
    length = stripe.shape[dimension]
    differ = part_of(stripe, 1, length, dimension) - part_of(stripe, 0, length - 1, dimension)
    slopes = minmod(
        part_of(differ, 0, length - 2, dimension), part_of(differ, 1, length - 1, dimension)
    )
    left_side = part_of(stripe, 1, length - 2, dimension) + 0.5 * part_of(
        slopes, 0, length - 3, dimension
    )
    rights = part_of(stripe, 2, length - 1, dimension) - 0.5 * part_of(
        slopes, 1, length - 2, dimension
    )
    velocity = stripe[velocity_index : velocity_index + 1]
    face_speed = 0.5 * (
        part_of(velocity, 1, length - 2, dimension) + part_of(velocity, 2, length - 1, dimension)
    )
    conduct = jnp.exp(0.5 * jnp.tanh(stripe[5:6]))
    face_conduct = 0.5 * (
        part_of(conduct, 1, length - 2, dimension) + part_of(conduct, 2, length - 1, dimension)
    )
    fluxes = jnp.maximum(face_speed, 0.0) * left_side + jnp.minimum(face_speed, 0.0) * rights
    gradient = spread * face_conduct * part_of(differ, 1, length - 2, dimension)
    net_flux = gradient - courant * fluxes
    return part_of(net_flux, 1, length - 3, dimension) - part_of(net_flux, 0, length - 4, dimension)


def advance(zstripe, ystripe, xstripe, diffusivity):
    spread = diffusivity.reshape(-1, 1, 1, 1)
    center = part_of(xstripe, 2, xstripe.shape[3] - 2, 3)
    total = center + along(zstripe, 1, 2, spread)
    total = total + along(ystripe, 2, 1, spread)
    return total + along(xstripe, 3, 0, spread)


def pick_row(values, position):
    return lax.dynamic_index_in_dim(
        values, jnp.clip(position, 0, values.shape[0] - 1), 0, keepdims=False
    )


def local(old_state, old_owner, old_slot, diffusivity):
    device = lax.axis_index(("gx", "gy"))
    count_devices = lax.axis_size("gx") * lax.axis_size("gy")
    slot_total = old_state.shape[0]
    first_label = device * CAP
    owners = lax.dynamic_slice_in_dim(old_owner, first_label, CAP, 0)
    slots_here = lax.dynamic_slice_in_dim(old_slot, first_label, CAP, 0)
    below = (device - 1 + count_devices) % count_devices
    from_lower = shifted(old_state[slot_total - DRIFT :], ("gx", "gy"), 1)
    from_upper = shifted(old_state[:DRIFT], ("gx", "gy"), -1)
    lower_base = slot_total - DRIFT
    placed = []
    for column in range(CAP):
        owner_box = owners[column]
        slot_box = slots_here[column]
        lower_row = pick_row(from_lower, slot_box - lower_base)
        upper_row = pick_row(from_upper, slot_box)
        local_row = pick_row(old_state, slot_box)
        placed.append(
            jnp.where(
                owner_box == device, local_row, jnp.where(owner_box == below, lower_row, upper_row)
            )
        )
    region = (
        jnp.stack(placed)
        .reshape(CAP, F, B, B, B)
        .transpose(1, 2, 3, 0, 4)
        .reshape(F, B, B, CAP * B)
    )
    padded = padded_2(region, (("gx", 1), ("gy", 2)), 2)
    outer_index = lax.axis_index("gx")
    inner_index = lax.axis_index("gy")
    outer_last = lax.axis_size("gx") - 1
    inner_last = lax.axis_size("gy") - 1
    z_bottom = jnp.where(
        outer_index == 0, jnp.concatenate([region[:, :1], region[:, :1]], 1), padded[:, :2, 2:-2, :]
    )
    z_top = jnp.where(
        outer_index == outer_last,
        jnp.concatenate([region[:, -1:], region[:, -1:]], 1),
        padded[:, -2:, 2:-2, :],
    )
    y_bottom = jnp.where(
        inner_index == 0,
        jnp.concatenate([region[:, :, :1], region[:, :, :1]], 2),
        padded[:, 2:-2, :2, :],
    )
    y_top = jnp.where(
        inner_index == inner_last,
        jnp.concatenate([region[:, :, -1:], region[:, :, -1:]], 2),
        padded[:, 2:-2, -2:, :],
    )
    zstripe = jnp.concatenate([z_bottom, region, z_top], 1)
    ystripe = jnp.concatenate([y_bottom, region, y_top], 2)
    xstripe = jnp.concatenate(
        [region[..., :1], region[..., :1], region, region[..., -1:], region[..., -1:]], 3
    )
    updated = advance(zstripe, ystripe, xstripe, diffusivity)
    updated = updated.reshape(F, B, B, CAP, B).transpose(3, 0, 1, 2, 4)
    return updated.reshape(CAP, F, B * B * B)


def solution(mesh):
    placed = (P(("gx", "gy"), None, None), P(), P(), P())
    return jax.shard_map(
        local, mesh=mesh, in_specs=placed, out_specs=P(("gx", "gy"), None, None), check_vma=False
    )
```

profile of v0, /device:TPU:0, one launch (start us, length us, event | category | flops | bytes accessed | tf_op | source)
XLA Modules:
  0.0 219.3 jit_solution(2986664481189731109)
XLA Ops:
  0.0 6.1 %fusion.48 = (f32[2,6,32768]{2,0,1:T(2,128)S(1)}, f32[2,6,32768]{2,0,1:T(2,128)S(1)}) fusion(f32[8,6,32768]{2,0,1:T(8,128)} %param.4), kind=kLoop, calls=%fused_computation.108 | loop fusion | bytes 6291456 | tf_op jit(solution)/shard_map/slice | solution.py:92
  6.1 2.3 %copy.18 = f32[2,6,32768]{2,1,0:T(8,128)} copy(f32[2,6,32768]{2,0,1:T(2,128)S(1)} %get-tuple-element.16) | data formatting | bytes 3145728
  8.3 6.4 %collective-permute-start.1 = (f32[2,6,32768]{2,1,0:T(8,128)}, f32[2,6,32768]{2,1,0:T(8,128)S(1)}, u32[]{:S(2)}, u32[]{:S(2)}) collective-permute-start(f32[2,6,32768]{2,1,0:T(8,128)} %copy.18), channel_id=1, source_target_pairs={{1,0},{2,1},{3,2},{4,3},{5,4},{6,5},{7,6},{8,7},{9,8},{10,9},{11,1... | collective-permute-start | bytes 4718600 | tf_op jit(solution)/shard_map/ppermute | solution.py:18
  14.7 2.3 %copy.17 = f32[2,6,32768]{2,1,0:T(8,128)} copy(f32[2,6,32768]{2,0,1:T(2,128)S(1)} %get-tuple-element.15) | data formatting | bytes 3145728
  20.5 12.9 %constant_dynamic-slice_fusion.3 = (f32[1,6,32768]{2,0,1:T(1,128)S(1)}, f32[1,6,32768]{2,0,1:T(1,128)}, f32[1,6,32768]{2,0,1:T(1,128)}, f32[1,6,32768]{2,0,1:T(1,128)}) fusion(f32[8,6,32768]{2,0,1:T(8,128)} %param.4, s32[]{:T(128)} %bitcast.1, s32[]{:T(128)} %bitcast.9, s32[]{:T(128)} %bitcast.5, s32[]{:T(128)} %bitcast.13), kind=kLoop, calls=%fused_computation.107 | loop fusion | bytes 6291472 | tf_op jit(solution)/shard_map/jit(dynamic_index_in_dim)/dynamic_slice | solution.py:79
  42.0 17.6 %collective-permute-done.1 = f32[2,6,32768]{2,1,0:T(8,128)S(1)} collective-permute-done((f32[2,6,32768]{2,1,0:T(8,128)}, f32[2,6,32768]{2,1,0:T(8,128)S(1)}, u32[]{:S(2)}, u32[]{:S(2)}) %collective-permute-start.1) | collective-permute-done | bytes 1572896 | tf_op jit(solution)/shard_map/ppermute | solution.py:18
  59.6 2.5 %collective-permute-done = f32[2,6,32768]{2,1,0:T(8,128)} collective-permute-done((f32[2,6,32768]{2,1,0:T(8,128)}, f32[2,6,32768]{2,1,0:T(8,128)}, u32[]{:S(2)}, u32[]{:S(2)}) %collective-permute-start) | collective-permute-done | bytes 1572896 | tf_op jit(solution)/shard_map/ppermute | solution.py:18
  62.1 5.5 %copy_select_fusion.3 = (f32[1,6,32768]{2,1,0:T(8,128)}, f32[1,6,32768]{2,1,0:T(8,128)}, f32[1,6,32768]{2,1,0:T(8,128)}) fusion(f32[1,6,32768]{2,0,1:T(1,128)S(1)} %get-tuple-element.11, f32[2,6,32768]{2,1,0:T(8,128)S(1)} %collective-permute-done.1, s32[]{:T(128)} %bitcast.3, f32[2,6,32768]{2,1,0:T(8,128)} %collective-permute-done, s32[]{:T(128)} %bitcast.2, ...), kind=kLoop, calls=%fused_computation.74 | loop fusion | flops 1179648 | bytes 9437214 | tf_op jit(solution)/shard_map/jit(_where)/select_n | solution.py:103
  67.5 2.2 %stack.18 = f32[1,6,32,32,32]{4,3,2,0,1:T(8,128)S(1)} reshape(f32[1,6,32768]{2,1,0:T(8,128)} %get-tuple-element.18) | data formatting | bytes 1572864 | tf_op jit(solution)/shard_map/stack | solution.py:108
  69.8 3.9 %stack.17 = f32[1,6,32,32,32]{4,3,2,0,1:T(8,128)} reshape(f32[1,6,32768]{2,1,0:T(8,128)} %get-tuple-element.19) | data formatting | bytes 1572864 | tf_op jit(solution)/shard_map/stack | solution.py:108
  73.7 3.3 %copy_select_fusion.2 = f32[1,6,32768]{2,1,0:T(8,128)} fusion(f32[1,6,32768]{2,0,1:T(1,128)} %get-tuple-element.13, f32[2,6,32768]{2,1,0:T(8,128)} %copy-done.5, s32[]{:T(128)} %bitcast.7, f32[2,6,32768]{2,1,0:T(8,128)} %collective-permute-done, s32[]{:T(128)} %bitcast.6, pred[]{:T(512)S(6)} %eq.41, pred[]{:T(512)S(6)} %eq.40), kind=kLoop, calls=%fused_computation.73 | loop fusion | flops 393216 | bytes 3145738 | tf_op jit(solution)/shard_map/jit(_where)/select_n | solution.py:103
  76.9 3.9 %stack.16 = f32[1,6,32,32,32]{4,3,2,0,1:T(8,128)} reshape(f32[1,6,32768]{2,1,0:T(8,128)} %copy_select_fusion.2) | data formatting | bytes 1572864 | tf_op jit(solution)/shard_map/stack | solution.py:108
  80.8 3.9 %stack.15 = f32[1,6,32,32,32]{4,3,2,0,1:T(8,128)} reshape(f32[1,6,32768]{2,1,0:T(8,128)} %get-tuple-element.17) | data formatting | bytes 1572864 | tf_op jit(solution)/shard_map/stack | solution.py:108
  84.7 5.4 %maximum_bitcast_fusion = f32[6,32,32,4,32]{4,2,1,3,0:T(8,128)S(1)} fusion(f32[1,6,32,32,32]{4,3,2,0,1:T(8,128)S(1)} %stack.18, f32[1,6,32,32,32]{4,3,2,0,1:T(8,128)} %stack.17, f32[1,6,32,32,32]{4,3,2,0,1:T(8,128)} %stack.16, f32[1,6,32,32,32]{4,3,2,0,1:T(8,128)} %stack.15), kind=kLoop, calls=%fused_computation | loop fusion | flops 2359296 | bytes 6291456 | tf_op jit(solution)/shard_map/transpose | solution.py:110
  90.1 11.9 %copy.14 = f32[6,32,32,4,32]{4,3,2,1,0:T(4,128)} copy(f32[6,32,32,4,32]{4,2,1,3,0:T(8,128)S(1)} %maximum_bitcast_fusion) | data formatting | bytes 6291456 | tf_op jit(solution)/shard_map/transpose | solution.py:110
  102.0 9.2 %reshape.64 = f32[6,32,32,128]{3,2,1,0:T(8,128)S(1)} reshape(f32[6,32,32,4,32]{4,3,2,1,0:T(4,128)} %copy.14) | data formatting | bytes 6291456 | tf_op jit(solution)/shard_map/reshape | solution.py:111
  112.3 1.7 copy-done
  115.0 9.1 %fusion.9 = f32[6,32,32,131]{3,2,1,0:T(8,128)} fusion(f32[6,32,32,1]{3,2,1,0:T(8,128)S(1)} %get-tuple-element.29, f32[6,32,32,1]{3,2,1,0:T(8,128)S(1)} %get-tuple-element.28, f32[6,32,32,128]{3,2,1,0:T(8,128)S(1)} %reshape.64), kind=kLoop, calls=%fused_computation.20 | loop fusion | flops 5634048 | bytes 6414336 | tf_op jit(solution)/shard_map/sub | solution.py:46
  124.1 12.5 %concatenate.66 = f32[6,32,32,132]{3,2,1,0:T(8,128)} concatenate(f32[6,32,32,1]{3,2,1,0:T(8,128)} %copy-done, f32[6,32,32,1]{3,2,1,0:T(8,128)} %copy-done, f32[6,32,32,128]{3,2,1,0:T(8,128)S(1)} %reshape.64, f32[6,32,32,1]{3,2,1,0:T(8,128)} %copy-done.2, f32[6,32,32,1]{3,2,1,0:T(8,128)} %copy-done.2), dimensions={3} | concatenate | bytes 6488064 | tf_op jit(solution)/shard_map/concatenate | solution.py:138
  136.6 2.7 %maximum_bitcast_fusion.1 = (f32[32,32,129]{2,1,0:T(8,128)S(1)}, f32[1,32,32,129]{3,2,1,0:T(8,128)}) fusion(f32[6,32,32,1]{3,2,1,0:T(8,128)} %copy-done.2, f32[6,32,32,128]{3,2,1,0:T(8,128)S(1)} %reshape.64, f32[6,32,32,1]{3,2,1,0:T(8,128)} %copy-done), kind=kLoop, calls=%fused_computation.76 | loop fusion | flops 660480 | bytes 4251648 | tf_op jit(solution)/shard_map/mul | solution.py:64
  140.1 6.9 %minimum_multiply_fusion = f32[6,32,32,130]{3,2,1,0:T(8,128)} fusion(f32[6,32,32,131]{3,2,1,0:T(8,128)S(1)} %copy-done.4), kind=kLoop, calls=%fused_computation.24 | loop fusion | flops 6389760 | bytes 9584640 | tf_op jit(solution)/shard_map/mul | solution.py:36
  150.1 4.6 %collective-permute-start.2 = (f32[6,2,32,128]{3,2,1,0:T(8,128)S(1)}, f32[6,2,32,128]{3,2,1,0:T(8,128)S(1)}, u32[]{:S(2)}, u32[]{:S(2)}) collective-permute-start(f32[6,2,32,128]{3,2,1,0:T(8,128)S(1)} %get-tuple-element.27), channel_id=1, source_target_pairs={{0,8},{8,16},{16,24},{1,9},{9,17},{17,25},{2,10},{10,18},{18,26},{... | collective-permute-start | bytes 589832 | tf_op jit(solution)/shard_map/ppermute | solution.py:26
  154.6 1.9 fusion.32
  156.6 10.7 %fusion.4 = f32[6,32,32,129]{3,2,1,0:T(8,128)} fusion(f32[6,32,32,1]{3,2,1,0:T(8,128)S(1)} %copy-done.3, f32[6,32,32,128]{3,2,1,0:T(8,128)S(1)} %reshape.64, f32[6,32,32,1]{3,2,1,0:T(8,128)S(1)} %copy-done.1, f32[6,32,32,130]{3,2,1,0:T(8,128)} %minimum_multiply_fusion, f32[6,32,32,131]{3,2,1,0:T(8,128)} %fusion.9, f32[32,32,129]{2,1,0:T(8,128)S(1)} %get-tuple-element.43, ...), kind=kLoop, calls=%fused_computation.15 | loop fusion | flops 10303488 | bytes 17461272 | tf_op jit(solution)/shard_map/sub | solution.py:66
  169.8 3.0 %collective-permute-start.4 = (f32[6,36,2,128]{3,2,1,0:T(2,128)S(1)}, f32[6,36,2,128]{3,2,1,0:T(2,128)S(1)}, u32[]{:S(2)}, u32[]{:S(2)}) collective-permute-start(f32[6,36,2,128]{3,2,1,0:T(2,128)S(1)} %get-tuple-element.20), channel_id=1, source_target_pairs={{0,1},{1,2},{2,3},{3,4},{4,5},{5,6},{6,7},{8,9},{9,10},{10,11},{11... | collective-permute-start | bytes 663560 | tf_op jit(solution)/shard_map/ppermute | solution.py:26
  174.9 2.5 %fusion.21 = f32[6,33,32,128]{3,2,1,0:T(8,128)S(1)} fusion(f32[6,34,32,128]{3,2,1,0:T(8,128)S(1)} %minimum_multiply_fusion.2, f32[6,2,32,128]{3,2,1,0:T(8,128)S(1)} %get-tuple-element.32, f32[6,32,32,128]{3,2,1,0:T(8,128)S(1)} %reshape.64, f32[6,2,32,128]{3,2,1,0:T(8,128)S(1)} %get-tuple-element.30, f32[6,35,32,128]{3,2,1,0:T(8,128)S(1)} %slice_subtract_fusion.1, ...), kind=kLoop, calls=%fused_computation.48 | loop fusion | flops 10543104 | bytes 18137112 | tf_op jit(solution)/shard_map/sub | solution.py:66
  179.2 2.8 %minimum_multiply_fusion.1 = f32[6,32,34,128]{3,2,1,0:T(8,128)S(1)} fusion(f32[6,32,35,128]{3,2,1,0:T(8,128)S(1)} %slice_subtract_fusion), kind=kLoop, calls=%fused_computation.39 | loop fusion | flops 6684672 | bytes 10027008 | tf_op jit(solution)/shard_map/mul | solution.py:36
  182.2 2.8 %fusion.14 = f32[6,32,33,128]{3,2,1,0:T(8,128)S(1)} fusion(f32[6,32,34,128]{3,2,1,0:T(8,128)S(1)} %minimum_multiply_fusion.1, f32[6,32,2,128]{3,2,1,0:T(2,128)S(1)} %slice_select_fusion, f32[6,32,32,128]{3,2,1,0:T(8,128)S(1)} %reshape.64, f32[6,32,2,128]{3,2,1,0:T(2,128)S(1)} %slice_select_fusion.1, f32[6,32,35,128]{3,2,1,0:T(8,128)S(1)} %slice_subtract_fusion, ...), kind=kLoop, calls=%fused_computation.30 | loop fusion | flops 10543104 | bytes 18137112 | tf_op jit(solution)/shard_map/sub | solution.py:66
  185.1 3.2 %fusion.24 = f32[6,32,32,128]{3,2,1,0:T(8,128)} fusion(f32[6,32,32,129]{3,2,1,0:T(8,128)S(1)} %bitcast.45, f32[6,32,33,128]{3,2,1,0:T(8,128)S(1)} %fusion.14, f32[6,32,32,128]{3,2,1,0:T(8,128)S(1)} %reshape.64, f32[6,33,32,128]{3,2,1,0:T(8,128)S(1)} %fusion.21), kind=kLoop, calls=%fused_computation.56 | loop fusion | flops 4718592 | bytes 25165824 | tf_op jit(solution)/shard_map/add | solution.py:75
  188.2 9.9 %reshape.65 = f32[6,32,32,4,32]{4,3,2,1,0:T(4,128)} reshape(f32[6,32,32,128]{3,2,1,0:T(8,128)} %fusion.24) | data formatting | bytes 6291456 | tf_op jit(solution)/shard_map/reshape | solution.py:142
  198.2 10.9 %copy.15 = f32[4,6,32,32,32]{4,3,2,0,1:T(8,128)} copy(f32[4,6,32,32,32]{4,0,3,2,1:T(4,128)} %bitcast.43) | data formatting | bytes 6291456 | tf_op jit(solution)/shard_map/transpose | solution.py:142
  209.1 10.0 %reshape.66 = f32[4,6,32768]{2,0,1:T(4,128)} reshape(f32[4,6,32,32,32]{4,3,2,0,1:T(8,128)} %copy.15) | data formatting | bytes 6291456 | tf_op jit(solution)/shard_map/reshape | solution.py:143
  (55 shorter events, 14.0 us)
Async XLA Ops:
  6.1 11.1 %copy-start.7 = (s32[128]{0:T(128)S(1)}, s32[128]{0:T(128)}, u32[]{:S(2)}) copy-start(s32[128]{0:T(128)} %param.6) | copy-start | bytes 1540
  8.3 51.3 %collective-permute-start.1 = (f32[2,6,32768]{2,1,0:T(8,128)}, f32[2,6,32768]{2,1,0:T(8,128)S(1)}, u32[]{:S(2)}, u32[]{:S(2)}) collective-permute-start(f32[2,6,32768]{2,1,0:T(8,128)} %copy.18), channel_id=1, source_target_pairs={{1,0},{2,1},{3,2},{4,3},{5,4},{6,5},{7,6},{8,7},{9,8},{10,9},{11,1... | collective-permute-start | bytes 4718600 | tf_op jit(solution)/shard_map/ppermute | solution.py:18
  17.0 17.7 %copy-start.8 = (s32[128]{0:T(128)S(1)}, s32[128]{0:T(128)}, u32[]{:S(2)}) copy-start(s32[128]{0:T(128)} %param.5) | copy-start | bytes 1540
  17.0 45.1 %collective-permute-start = (f32[2,6,32768]{2,1,0:T(8,128)}, f32[2,6,32768]{2,1,0:T(8,128)}, u32[]{:S(2)}, u32[]{:S(2)}) collective-permute-start(f32[2,6,32768]{2,1,0:T(8,128)} %copy.17), channel_id=1, source_target_pairs={{31,0},{0,1},{1,2},{2,3},{3,4},{4,5},{5,6},{6,7},{7,8},{8,9},{9,10... | collective-permute-start | bytes 4718600 | tf_op jit(solution)/shard_map/ppermute | solution.py:18
  59.6 7.9 %copy-start.5 = (f32[2,6,32768]{2,1,0:T(8,128)}, f32[2,6,32768]{2,1,0:T(8,128)S(1)}, u32[]{:S(2)}) copy-start(f32[2,6,32768]{2,1,0:T(8,128)S(1)} %collective-permute-done.1) | copy-start | bytes 4718596
  112.3 1.7 copy-start
  112.3 2.7 %copy-start.2 = (f32[6,32,32,1]{3,2,1,0:T(8,128)}, f32[6,32,32,1]{3,2,1,0:T(8,128)S(1)}, u32[]{:S(2)}) copy-start(f32[6,32,32,1]{3,2,1,0:T(8,128)S(1)} %get-tuple-element.29) | copy-start | bytes 73732
  136.6 3.5 %copy-start.4 = (f32[6,32,32,131]{3,2,1,0:T(8,128)S(1)}, f32[6,32,32,131]{3,2,1,0:T(8,128)}, u32[]{:S(2)}) copy-start(f32[6,32,32,131]{3,2,1,0:T(8,128)} %fusion.9) | copy-start | bytes 9658372
  147.0 9.5 %copy-start.1 = (f32[6,32,32,1]{3,2,1,0:T(8,128)S(1)}, f32[6,32,32,1]{3,2,1,0:T(8,128)}, u32[]{:S(2)}) copy-start(f32[6,32,32,1]{3,2,1,0:T(8,128)} %copy-done) | copy-start | bytes 73732
  147.0 9.6 %copy-start.3 = (f32[6,32,32,1]{3,2,1,0:T(8,128)S(1)}, f32[6,32,32,1]{3,2,1,0:T(8,128)}, u32[]{:S(2)}) copy-start(f32[6,32,32,1]{3,2,1,0:T(8,128)} %copy-done.2) | copy-start | bytes 73732
  147.0 9.6 %copy-start.6 = (f32[6]{0:T(128)S(1)}, f32[6]{0:T(128)}, u32[]{:S(2)}) copy-start(f32[6]{0:T(128)} %param.7) | copy-start | bytes 76
  148.6 19.0 %collective-permute-start.3 = (f32[6,2,32,128]{3,2,1,0:T(8,128)S(1)}, f32[6,2,32,128]{3,2,1,0:T(8,128)S(1)}, u32[]{:S(2)}, u32[]{:S(2)}) collective-permute-start(f32[6,2,32,128]{3,2,1,0:T(8,128)S(1)} %get-tuple-element.26), channel_id=1, source_target_pairs={{8,0},{16,8},{24,16},{9,1},{17,9},{25,17},{10,2},{18,10},{26,18},{... | collective-permute-start | bytes 589832 | tf_op jit(solution)/shard_map/ppermute | solution.py:29
  150.1 17.2 %collective-permute-start.2 = (f32[6,2,32,128]{3,2,1,0:T(8,128)S(1)}, f32[6,2,32,128]{3,2,1,0:T(8,128)S(1)}, u32[]{:S(2)}, u32[]{:S(2)}) collective-permute-start(f32[6,2,32,128]{3,2,1,0:T(8,128)S(1)} %get-tuple-element.27), channel_id=1, source_target_pairs={{0,8},{8,16},{16,24},{1,9},{9,17},{17,25},{2,10},{10,18},{18,26},{... | collective-permute-start | bytes 589832 | tf_op jit(solution)/shard_map/ppermute | solution.py:26
  168.5 8.9 %collective-permute-start.5 = (f32[6,36,2,128]{3,2,1,0:T(2,128)S(1)}, f32[6,36,2,128]{3,2,1,0:T(2,128)S(1)}, u32[]{:S(2)}, u32[]{:S(2)}) collective-permute-start(f32[6,36,2,128]{3,2,1,0:T(2,128)S(1)} %get-tuple-element.21), channel_id=1, source_target_pairs={{1,0},{2,1},{3,2},{4,3},{5,4},{6,5},{7,6},{9,8},{10,9},{11,10},{12... | collective-permute-start | bytes 663560 | tf_op jit(solution)/shard_map/ppermute | solution.py:29
  169.8 7.8 %collective-permute-start.4 = (f32[6,36,2,128]{3,2,1,0:T(2,128)S(1)}, f32[6,36,2,128]{3,2,1,0:T(2,128)S(1)}, u32[]{:S(2)}, u32[]{:S(2)}) collective-permute-start(f32[6,36,2,128]{3,2,1,0:T(2,128)S(1)} %get-tuple-element.20), channel_id=1, source_target_pairs={{0,1},{1,2},{2,3},{3,4},{4,5},{5,6},{6,7},{8,9},{9,10},{10,11},{11... | collective-permute-start | bytes 663560 | tf_op jit(solution)/shard_map/ppermute | solution.py:26
  182.0 3.0 %slice-start = ((s8[6291456]{0:T(1024)(128)(4,1)}), s8[4194304]{0:T(1024)(128)(4,1)S(1)}, s32[]{:S(2)}) async-start(s8[6291456]{0:T(1024)(128)(4,1)} %bitcast.44), calls=%async_computation | async-start | bytes 8388608
  182.2 2.9 %slice-start.1 = ((s8[6291456]{0:T(1024)(128)(4,1)}), s8[2097152]{0:T(1024)(128)(4,1)S(1)}, s32[]{:S(2)}) async-start(s8[6291456]{0:T(1024)(128)(4,1)} %bitcast.44), calls=%async_computation.1 | async-start | bytes 4194304
where the time goes:
time: 224 us; the launch traced here: 219 us
  local copies, waits for them, and re-layouts  108 us (48%)
  other arithmetic  63 us (28%)
  waiting for transfers between devices  20.1 us (9%)
  starting transfers between devices  16.8 us (8%)
  between operations  11.1 us (5%)
    ppermute x2, waiting for transfers between devices, shifted(): return lax.ppermute(block, axis, route)  20 us
    sub x3, other arithmetic, along(): net_flux = gradient - courant * fluxes  16 us
    another operation x4, local copies, waits for them, and re-layouts, local(): jnp.stack(placed).reshape(CAP, F, B, B, B).transpose(1, 2, 3, 0, 4)  13.9 us
    dynamic_slice x1, local copies, waits for them, and re-layouts, pick_row(): lax.dynamic_index_in_dim(values, jnp.clip(position, 0, values.shape[0] -...  12.9 us
    concatenate x1, local copies, waits for them, and re-layouts, local(): jnp.concatenate([region[..., :1], region[..., :1], region, region[..., -1...  12.5 us
    transpose x1, local copies, waits for them, and re-layouts, local(): region = jnp.stack(placed).reshape(CAP, F, B, B, B).transpose(1, 2, 3, 0,...  11.9 us
    mul x3, other arithmetic, minmod(): 0.5 * (jnp.sign(former) + jnp.sign(latter))  11 us
    transpose x1, local copies, waits for them, and re-layouts, local(): updated = updated.reshape(F, B, B, CAP, B).transpose(3, 0, 1, 2, 4)  10.9 us
  transfers between devices with their start and end apart: 6, of which 2 were waited for; matrix products, arithmetic and copies ran while one was open for 16% of the time, Pallas kernels for 0%

commit v1 on v0

v1 whole, which is shorter than its diff:
```python
import jax
import jax.numpy as jnp
from jax import lax
from jax.experimental import pallas as pl
from jax.experimental.pallas import tpu as pltpu
from jax.sharding import PartitionSpec as P

F = 6
CAP = 4
CHUNKS = 8
TILES = 8
PLANE = 1024
MESH = pl.DeviceIdType.MESH


def kernel(
    n_gx, n_gy, owner_ref, diff_ref, state_ref, out_ref,
    held, send, recv, q, cond, acc, wz, cz, wy, cy, wx, cx,
    zsend, zrecv, ysend, yrecv,
    in_sem, move_send, move_recv, z_send, z_recv, y_send, y_recv,
):
    gx = lax.axis_index("gx")
    gy = lax.axis_index("gy")
    count = n_gx * n_gy
    me = gx * n_gy + gy
    above = lax.rem(me + 1, count)
    below = lax.rem(me + count - 1, count)
    ring = ((above // n_gy, lax.rem(above, n_gy)), (below // n_gy, lax.rem(below, n_gy)))

    def in_copy(k, part):
        cells = pl.ds(pl.multiple_of((k + 8 * part) * PLANE, PLANE), PLANE)
        return pltpu.make_async_copy(
            state_ref.at[:, :, cells], held.at[:, :, cells], in_sem.at[k, part]
        )

    def start_in(k, _):
        for part in range(4):
            in_copy(k, part).start()
        return 0

    lax.fori_loop(0, CHUNKS, start_in, 0)

    barrier = pltpu.get_barrier_semaphore()
    for target in ring:
        pl.semaphore_signal(barrier, inc=1, device_id=target, device_id_type=MESH)

    @pl.when(gx > 0)
    def _():
        pl.semaphore_signal(barrier, inc=1, device_id=(gx - 1, gy), device_id_type=MESH)

    @pl.when(gx < n_gx - 1)
    def _():
        pl.semaphore_signal(barrier, inc=1, device_id=(gx + 1, gy), device_id_type=MESH)

    pl.semaphore_wait(
        barrier, 2 + (gx > 0).astype(jnp.int32) + (gx < n_gx - 1).astype(jnp.int32)
    )

    row = lax.broadcasted_iota(jnp.int32, (8, 128), 0)
    lane = lax.broadcasted_iota(jnp.int32, (8, 128), 1)
    box = row % 4
    col = lane % 32

    def sub(values, shift):
        return pltpu.roll(values, shift % 8, 0)

    def turn(values, shift):
        return pltpu.roll(values, shift % 128, 1)

    def tile_of(f, k, part, t):
        start = pl.multiple_of((k + 8 * part) * PLANE + t * 128, 128)
        return held[f, :, pl.ds(start, 128)]

    def move(way, k):
        return pltpu.make_async_remote_copy(
            src_ref=send.at[way, k],
            dst_ref=recv.at[way, k],
            send_sem=move_send.at[way, k],
            recv_sem=move_recv.at[way, k],
            device_id=ring[way],
            device_id_type=MESH,
        )

    def pack(k, _):
        for part in range(4):
            in_copy(k, part).wait()

        def field(f, _):
            for t in range(TILES):
                a, b, c, d = (tile_of(f, k, part, t) for part in range(4))
                a2, c6 = sub(a, 2), sub(c, 6)
                up = jnp.where(
                    row < 4, jnp.where(row < 2, a2, sub(b, 4)), jnp.where(row < 6, c6, d)
                )
                down = jnp.where(
                    row < 4, jnp.where(row < 2, b, a2), jnp.where(row < 6, sub(d, 4), c6)
                )
                send[0, k, f, t] = up
                send[1, k, f, t] = down
            return 0

        lax.fori_loop(0, F, field, 0)
        move(0, k).start()
        move(1, k).start()
        return 0

    lax.fori_loop(0, CHUNKS, pack, 0)

    owners = jnp.zeros((8, 128), jnp.int32)
    for c in range(CAP):
        owners = jnp.where(box == c, owner_ref[me * CAP + c], owners)
    kept = owners == me

    def y_copy(way, k):
        return pltpu.make_async_remote_copy(
            src_ref=ysend.at[way, k],
            dst_ref=yrecv.at[way, k],
            send_sem=y_send.at[way, k],
            recv_sem=y_recv.at[way, k],
            device_id=(gx, gy + 1) if way == 0 else (gx, gy - 1),
            device_id_type=MESH,
        )

    def z_copy(way):
        return pltpu.make_async_remote_copy(
            src_ref=zsend.at[way],
            dst_ref=zrecv.at[way],
            send_sem=z_send.at[way],
            recv_sem=z_recv.at[way],
            device_id=(gx + 1, gy) if way == 0 else (gx - 1, gy),
            device_id_type=MESH,
        )

    def gather(k, _):
        move(0, k).wait_recv()
        move(1, k).wait_recv()

        def field(f, _):
            for t in range(TILES):
                a, b, c, d = (tile_of(f, k, part, t) for part in range(4))
                up = recv[0, k, f, t]
                down = recv[1, k, f, t]
                first = jnp.where(
                    kept,
                    jnp.where(row < 4, sub(a, 6), sub(c, 2)),
                    jnp.where(box < 2, up, down),
                )
                second = jnp.where(
                    kept,
                    jnp.where(row < 4, sub(b, 6), sub(d, 2)),
                    jnp.where(box < 2, sub(up, 6), sub(down, 2)),
                )
                q[f, k + 2, t + 1] = first
                q[f, k + 10, t + 1] = second
                if t == 0:
                    ysend[1, k, f] = jnp.where(lane < 64, first, turn(second, 64))
                if t == TILES - 1:
                    ysend[0, k, f] = jnp.where(lane < 64, turn(second, 64), first)
            return 0

        lax.fori_loop(0, F, field, 0)

        @pl.when(gy < n_gy - 1)
        def _():
            y_copy(0, k).start()

        @pl.when(gy > 0)
        def _():
            y_copy(1, k).start()

        return 0

    lax.fori_loop(0, CHUNKS, gather, 0)

    def pack_z(f, _):
        for t in range(1, TILES + 1):
            zsend[1, f, t - 1] = jnp.where(row < 4, q[f, 2, t], sub(q[f, 3, t], 4))
            zsend[0, f, t - 1] = jnp.where(row < 4, sub(q[f, 16, t], 4), q[f, 17, t])
        return 0

    lax.fori_loop(0, F, pack_z, 0)

    @pl.when(gx < n_gx - 1)
    def _():
        z_copy(0).start()

    @pl.when(gx > 0)
    def _():
        z_copy(1).start()

    def fill_y(k, _):
        @pl.when(gy > 0)
        def _():
            y_copy(0, k).wait_recv()

        @pl.when(gy < n_gy - 1)
        def _():
            y_copy(1, k).wait_recv()

        def field(f, _):
            lower = yrecv[0, k, f]
            upper = yrecv[1, k, f]
            for plane, low, high in (
                (k + 2, lower, upper), (k + 10, turn(lower, 64), turn(upper, 64))
            ):
                bottom = q[f, plane, 1]
                top = q[f, plane, TILES]
                q[f, plane, 0] = jnp.where(
                    gy == 0, jnp.where(lane < 96, turn(bottom, 64), turn(bottom, 96)), low
                )
                q[f, plane, TILES + 1] = jnp.where(
                    gy == n_gy - 1, jnp.where(lane < 32, turn(top, 32), turn(top, 64)), high
                )
            return 0

        lax.fori_loop(0, F, field, 0)
        return 0

    lax.fori_loop(0, CHUNKS, fill_y, 0)

    @pl.when(gx > 0)
    def _():
        z_copy(0).wait_recv()

    @pl.when(gx < n_gx - 1)
    def _():
        z_copy(1).wait_recv()

    def fill_z(f, _):
        for t in range(1, TILES + 1):
            lower = zrecv[0, f, t - 1]
            upper = zrecv[1, f, t - 1]
            z0, z1, z14, z15 = q[f, 2, t], q[f, 3, t], q[f, 16, t], q[f, 17, t]
            first = gx == 0
            last = gx == n_gx - 1
            q[f, 0, t] = jnp.where(row < 4, jnp.where(first, z0, lower), sub(z14, 4))
            q[f, 1, t] = jnp.where(row < 4, jnp.where(first, z0, sub(lower, 4)), sub(z15, 4))
            q[f, 18, t] = jnp.where(row < 4, sub(z0, 4), jnp.where(last, z15, sub(upper, 4)))
            q[f, 19, t] = jnp.where(row < 4, sub(z1, 4), jnp.where(last, z15, upper))
        return 0

    lax.fori_loop(0, F, fill_z, 0)

    def conduct(z, _):
        for t in range(TILES + 2):
            cond[z, t] = 0.5 * jnp.exp(0.5 * jnp.tanh(q[5, z, t]))
        return 0

    lax.fori_loop(1, 19, conduct, 0)

    def minmod(a, b):
        return jnp.maximum(jnp.minimum(a, b), jnp.minimum(jnp.maximum(a, b), 0.0))

    def face(w, c, spread, d, left, right):
        return spread * c * d - w * jnp.where(w > 0.0, left, right)

    def along_z(t, _):
        for i in range(17):
            wz[i] = 0.125 * (q[2, i + 1, t] + q[2, i + 2, t])
            cz[i] = cond[i + 1, t] + cond[i + 2, t]

        def field(f, _):
            spread = diff_ref[f]
            here = q[f, 1, t]
            d_low = here - q[f, 0, t]
            after = q[f, 2, t]
            d = after - here
            left = here + 0.5 * minmod(d_low, d)
            before = None
            for i in range(17):
                here = after
                after = q[f, i + 3, t]
                d_next = after - here
                half = 0.5 * minmod(d, d_next)
                net = face(wz[i], cz[i], spread, d, left, here - half)
                left = here + half
                d = d_next
                if i > 0:
                    acc[f, i - 1, t - 1] = base + (net - before)
                before = net
                base = here
            return 0

        lax.fori_loop(0, F, field, 0)
        return 0

    lax.fori_loop(1, TILES + 1, along_z, 0)

    edge_low = (box == 0) & (col == 0)
    edge_high = (box == 3) & (col == 31)

    def x_next(values):
        return jnp.where(col == 31, sub(turn(values, 31), -1), turn(values, -1))

    def x_back(values):
        return jnp.where(col == 0, sub(turn(values, -31), 1), turn(values, 1))

    def y_next(values, later):
        return turn(jnp.where(lane < 32, later, values), -32)

    def y_back(values, earlier):
        return turn(jnp.where(lane >= 96, earlier, values), 32)

    def along_yx(z, _):
        for t in range(TILES + 1):
            u, c = q[1, z, t], cond[z, t]
            wy[t] = 0.125 * (u + y_next(u, q[1, z, t + 1]))
            cy[t] = c + y_next(c, cond[z, t + 1])
        for t in range(1, TILES + 1):
            u, c = q[0, z, t], cond[z, t]
            wx[t] = 0.125 * (u + jnp.where(edge_high, u, x_next(u)))
            cx[t] = c + jnp.where(edge_high, c, x_next(c))

        def field(f, _):
            spread = diff_ref[f]
            vals = [q[f, z, t] for t in range(TILES + 2)]
            diffs = [
                y_next(vals[t], vals[min(t + 1, TILES + 1)]) - vals[t] for t in range(TILES + 2)
            ]
            halves = [
                0.5 * minmod(y_back(diffs[t], diffs[max(t - 1, 0)]), diffs[t])
                for t in range(TILES + 2)
            ]
            rights = [v - h for v, h in zip(vals, halves)]
            nets = [
                face(
                    wy[t], cy[t], spread, diffs[t], vals[t] + halves[t],
                    y_next(rights[t], rights[t + 1]),
                )
                for t in range(TILES + 1)
            ]
            for t in range(1, TILES + 1):
                total = acc[f, z - 2, t - 1] + (nets[t] - y_back(nets[t], nets[t - 1]))
                v = vals[t]
                d = jnp.where(edge_high, 0.0, x_next(v) - v)
                half = 0.5 * minmod(jnp.where(edge_low, 0.0, x_back(d)), d)
                right = jnp.where(edge_high, v, x_next(v - half))
                net = face(wx[t], cx[t], spread, d, v + half, right)
                low = jnp.where(edge_low, -0.25 * q[0, z, t] * v, x_back(net))
                total = total + (net - low)
                start = pl.multiple_of((z - 2) * PLANE + (t - 1) * 128, 128)
                out_ref[f, :, pl.ds(start, 128)] = total[:4]
                out_ref[f, :, pl.ds(start + 16 * PLANE, 128)] = total[4:]
            return 0

        lax.fori_loop(0, F, field, 0)
        return 0

    lax.fori_loop(2, 18, along_yx, 0)

    def finish(k, _):
        move(0, k).wait_send()
        move(1, k).wait_send()

        @pl.when(gy < n_gy - 1)
        def _():
            y_copy(0, k).wait_send()

        @pl.when(gy > 0)
        def _():
            y_copy(1, k).wait_send()

        return 0

    lax.fori_loop(0, CHUNKS, finish, 0)

    @pl.when(gx < n_gx - 1)
    def _():
        z_copy(0).wait_send()

    @pl.when(gx > 0)
    def _():
        z_copy(1).wait_send()


def solution(mesh):
    n_gx, n_gy = mesh.shape["gx"], mesh.shape["gy"]

    def local(old_state, old_owner, old_slot, diffusivity):
        def body(*refs):
            kernel(n_gx, n_gy, *refs)

        vmem = pltpu.VMEM
        dma = pltpu.SemaphoreType.DMA
        cells = old_state.shape[2]
        result = pl.pallas_call(
            body,
            out_shape=jax.ShapeDtypeStruct((F, CAP, cells), jnp.float32),
            in_specs=[
                pl.BlockSpec(memory_space=pltpu.SMEM),
                pl.BlockSpec(memory_space=pltpu.SMEM),
                pl.BlockSpec(memory_space=pl.ANY),
            ],
            out_specs=pl.BlockSpec(memory_space=pltpu.VMEM),
            scratch_shapes=[
                vmem((F, 8, cells), jnp.float32),
                vmem((2, CHUNKS, F, TILES, 8, 128), jnp.float32),
                vmem((2, CHUNKS, F, TILES, 8, 128), jnp.float32),
                vmem((F, 20, TILES + 2, 8, 128), jnp.float32),
                vmem((20, TILES + 2, 8, 128), jnp.float32),
                vmem((F, 16, TILES, 8, 128), jnp.float32),
                vmem((17, 8, 128), jnp.float32),
                vmem((17, 8, 128), jnp.float32),
                vmem((TILES + 2, 8, 128), jnp.float32),
                vmem((TILES + 2, 8, 128), jnp.float32),
                vmem((TILES + 2, 8, 128), jnp.float32),
                vmem((TILES + 2, 8, 128), jnp.float32),
                vmem((2, F, TILES, 8, 128), jnp.float32),
                vmem((2, F, TILES, 8, 128), jnp.float32),
                vmem((2, CHUNKS, F, 8, 128), jnp.float32),
                vmem((2, CHUNKS, F, 8, 128), jnp.float32),
                dma((CHUNKS, 4)),
                dma((2, CHUNKS)),
                dma((2, CHUNKS)),
                dma((2,)),
                dma((2,)),
                dma((2, CHUNKS)),
                dma((2, CHUNKS)),
            ],
            compiler_params=pltpu.CompilerParams(
                collective_id=0, has_side_effects=True, vmem_limit_bytes=56 * 2**20
            ),
        )(old_owner, diffusivity, jnp.transpose(old_state, (1, 0, 2)))
        return jnp.transpose(result, (1, 0, 2))

    placed = (P(("gx", "gy"), None, None), P(), P(), P())
    return jax.shard_map(
        local, mesh=mesh, in_specs=placed, out_specs=P(("gx", "gy"), None, None), check_vma=False
    )
```

time: 224 us -> 98.1 us (0.44); the launches traced: 219 us -> 97.9 us
  local copies, waits for them, and re-layouts: 108 us -> 3.76 us
  Pallas kernels: 0 us -> 94.1 us
  other arithmetic: 63 us -> 0 us
  waiting for transfers between devices: 20.1 us -> 0 us
  starting transfers between devices: 16.8 us -> 0 us
  between operations: 11.1 us -> 0.01 us
    pallas_call x0 -> x1, Pallas kernels: none -> 94.1 us  [local(): pl.pallas_call(body, out_shape=jax.ShapeDtypeStruct((F, CAP, cells), jnp....]
    reshape x3 -> x0, local copies, waits for them, and re-layouts: 29.1 us -> none  [the longest x1 10 us: local(): return updated.reshape(CAP, F, B * B * B)]
    sub x6 -> x0, other arithmetic: 26.2 us -> none  [the longest x3 16 us: along(): net_flux = gradient - courant * fluxes]
    transpose x2 -> x0, local copies, waits for them, and re-layouts: 22.8 us -> none  [the longest x1 11.9 us: local(): region = jnp.stack(placed).reshape(CAP, F, B, B, B).transpose(1, 2, 3, 0,...]
    ppermute x6 -> x0, waiting for transfers between devices: 20.1 us -> none  [the longest x2 20 us: shifted(): return lax.ppermute(block, axis, route)]
    ppermute x6 -> x0, starting transfers between devices: 16.8 us -> none  [the longest x2 7.6 us: padded_2(): lax.ppermute(lax.slice_in_dim(block, block.shape[dim] - width, None, axis...]
    mul x9 -> x0, other arithmetic: 16.1 us -> none  [the longest x3 11 us: minmod(): 0.5 * (jnp.sign(former) + jnp.sign(latter))]
    another operation x4 -> x0, local copies, waits for them, and re-layouts: 13.9 us -> none  [local(): jnp.stack(placed).reshape(CAP, F, B, B, B).transpose(1, 2, 3, 0, 4)]
  transfers between devices with their start and end apart: 6 -> 0, of which waited for: 2 -> 0; matrix products, arithmetic and copies ran while one was open for 16% -> 0% of each run, Pallas kernels for 0% -> 0%
where the time goes in v1:
time: 98.1 us; the launch traced here: 97.9 us
  Pallas kernels  94.1 us (96%)
  local copies, waits for them, and re-layouts  3.76 us (4%)
    pallas_call x1, Pallas kernels, local(): pl.pallas_call(body, out_shape=jax.ShapeDtypeStruct((F, CAP, cells), jnp....  94.1 us
    unnamed x1, local copies, waits for them, and re-layouts  3.76 us

profile of v1, /device:TPU:0, one launch (start us, length us, event | category | flops | bytes accessed | tf_op | source)
XLA Modules:
  0.0 97.9 jit_solution(18180341089746349552)
XLA Ops:
  0.0 94.1 %shard_map.37 = f32[6,4,32768]{2,1,0:T(4,128)} custom-call(s32[128]{0:T(128)} %refs_0_.1, f32[6]{0:T(128)} %refs_1_.1, f32[6,8,32768]{2,1,0:T(8,128)} %bitcast.3), custom_call_target="tpu_custom_call" | custom-call | tf_op jit(solution)/shard_map/pallas_call | solution.py:386
  94.2 3.8 %copy.5 = f32[4,6,32768]{2,0,1:T(4,128)} copy(f32[4,6,32768]{2,0,1:T(4,128)} %bitcast.2) | data formatting | bytes 6291456

commit v2 on v1

--- a/solution.py
+++ b/solution.py
@@ -131,7 +131,7 @@
             device_id_type=MESH,
         )
 
-    def gather(k, _):
+    def gather(k):
         move(0, k).wait_recv()
         move(1, k).wait_recv()
 
@@ -168,27 +168,7 @@
         def _():
             y_copy(1, k).start()
 
-        return 0
-
-    lax.fori_loop(0, CHUNKS, gather, 0)
-
-    def pack_z(f, _):
-        for t in range(1, TILES + 1):
-            zsend[1, f, t - 1] = jnp.where(row < 4, q[f, 2, t], sub(q[f, 3, t], 4))
-            zsend[0, f, t - 1] = jnp.where(row < 4, sub(q[f, 16, t], 4), q[f, 17, t])
-        return 0
-
-    lax.fori_loop(0, F, pack_z, 0)
-
-    @pl.when(gx < n_gx - 1)
-    def _():
-        z_copy(0).start()
-
-    @pl.when(gx > 0)
-    def _():
-        z_copy(1).start()
-
-    def fill_y(k, _):
+    def fill_y(k):
         @pl.when(gy > 0)
         def _():
             y_copy(0, k).wait_recv()
@@ -214,9 +194,105 @@
             return 0
 
         lax.fori_loop(0, F, field, 0)
-        return 0
-
-    lax.fori_loop(0, CHUNKS, fill_y, 0)
+
+    def conduct(z):
+        for t in range(TILES + 2):
+            cond[z, t] = 0.5 * jnp.exp(0.5 * jnp.tanh(q[5, z, t]))
+
+    def minmod(a, b):
+        return jnp.maximum(jnp.minimum(a, b), jnp.minimum(jnp.maximum(a, b), 0.0))
+
+    def face(w, c, spread, d, left, right):
+        return spread * c * d - w * jnp.where(w > 0.0, left, right)
+
+    edge_low = (box == 0) & (col == 0)
+    edge_high = (box == 3) & (col == 31)
+
+    def x_next(values):
+        return jnp.where(col == 31, sub(turn(values, 31), -1), turn(values, -1))
+
+    def x_back(values):
+        return jnp.where(col == 0, sub(turn(values, -31), 1), turn(values, 1))
+
+    def y_next(values, later):
+        return turn(jnp.where(lane < 32, later, values), -32)
+
+    def y_back(values, earlier):
+        return turn(jnp.where(lane >= 96, earlier, values), 32)
+
+    def along_yx(z):
+        conduct(z)
+        for t in range(TILES + 1):
+            u, c = q[1, z, t], cond[z, t]
+            wy[t] = 0.125 * (u + y_next(u, q[1, z, t + 1]))
+            cy[t] = c + y_next(c, cond[z, t + 1])
+        for t in range(1, TILES + 1):
+            u, c = q[0, z, t], cond[z, t]
+            wx[t] = 0.125 * (u + jnp.where(edge_high, u, x_next(u)))
+            cx[t] = c + jnp.where(edge_high, c, x_next(c))
+
+        def field(f, _):
+            spread = diff_ref[f]
+            vals = [q[f, z, t] for t in range(TILES + 2)]
+            diffs = [
+                y_next(vals[t], vals[min(t + 1, TILES + 1)]) - vals[t] for t in range(TILES + 2)
+            ]
+            halves = [
+                0.5 * minmod(y_back(diffs[t], diffs[max(t - 1, 0)]), diffs[t])
+                for t in range(TILES + 2)
+            ]
+            rights = [v - h for v, h in zip(vals, halves)]
+            nets = [
+                face(
+                    wy[t], cy[t], spread, diffs[t], vals[t] + halves[t],
+                    y_next(rights[t], rights[t + 1]),
+                )
+                for t in range(TILES + 1)
+            ]
+            for t in range(1, TILES + 1):
+                total = vals[t] + (nets[t] - y_back(nets[t], nets[t - 1]))
+                v = vals[t]
+                d = jnp.where(edge_high, 0.0, x_next(v) - v)
+                half = 0.5 * minmod(jnp.where(edge_low, 0.0, x_back(d)), d)
+                right = jnp.where(edge_high, v, x_next(v - half))
+                net = face(wx[t], cx[t], spread, d, v + half, right)
+                low = jnp.where(edge_low, -0.25 * q[0, z, t] * v, x_back(net))
+                total = total + (net - low)
+                acc[f, z - 2, t - 1] = total
+            return 0
+
+        lax.fori_loop(0, F, field, 0)
+
+    def update(k):
+        fill_y(k)
+        along_yx(k + 2)
+        along_yx(k + 10)
+
+    def step(k, _):
+        gather(k)
+        update(k - 1)
+        return 0
+
+    gather(0)
+    lax.fori_loop(1, CHUNKS, step, 0)
+
+    def pack_z(f, _):
+        for t in range(1, TILES + 1):
+            zsend[1, f, t - 1] = jnp.where(row < 4, q[f, 2, t], sub(q[f, 3, t], 4))
+            zsend[0, f, t - 1] = jnp.where(row < 4, sub(q[f, 16, t], 4), q[f, 17, t])
+        return 0
+
+    lax.fori_loop(0, F, pack_z, 0)
+
+    @pl.when(gx < n_gx - 1)
+    def _():
+        z_copy(0).start()
+
+    @pl.when(gx > 0)
+    def _():
+        z_copy(1).start()
+
+    update(CHUNKS - 1)
 
     @pl.when(gx > 0)
     def _():
@@ -241,18 +317,8 @@
 
     lax.fori_loop(0, F, fill_z, 0)
 
-    def conduct(z, _):
-        for t in range(TILES + 2):
-            cond[z, t] = 0.5 * jnp.exp(0.5 * jnp.tanh(q[5, z, t]))
-        return 0
-
-    lax.fori_loop(1, 19, conduct, 0)
-
-    def minmod(a, b):
-        return jnp.maximum(jnp.minimum(a, b), jnp.minimum(jnp.maximum(a, b), 0.0))
-
-    def face(w, c, spread, d, left, right):
-        return spread * c * d - w * jnp.where(w > 0.0, left, right)
+    conduct(1)
+    conduct(18)
 
     def along_z(t, _):
         for i in range(17):
@@ -276,77 +342,17 @@
                 left = here + half
                 d = d_next
                 if i > 0:
-                    acc[f, i - 1, t - 1] = base + (net - before)
+                    total = acc[f, i - 1, t - 1] + (net - before)
+                    start = pl.multiple_of((i - 1) * PLANE + (t - 1) * 128, 128)
+                    out_ref[f, :, pl.ds(start, 128)] = total[:4]
+                    out_ref[f, :, pl.ds(start + 16 * PLANE, 128)] = total[4:]
                 before = net
-                base = here
             return 0
 
         lax.fori_loop(0, F, field, 0)
         return 0
 
     lax.fori_loop(1, TILES + 1, along_z, 0)
-
-    edge_low = (box == 0) & (col == 0)
-    edge_high = (box == 3) & (col == 31)
-
-    def x_next(values):
-        return jnp.where(col == 31, sub(turn(values, 31), -1), turn(values, -1))
-
-    def x_back(values):
-        return jnp.where(col == 0, sub(turn(values, -31), 1), turn(values, 1))
-
-    def y_next(values, later):
-        return turn(jnp.where(lane < 32, later, values), -32)
-
-    def y_back(values, earlier):
-        return turn(jnp.where(lane >= 96, earlier, values), 32)
-
-    def along_yx(z, _):
-        for t in range(TILES + 1):
-            u, c = q[1, z, t], cond[z, t]
-            wy[t] = 0.125 * (u + y_next(u, q[1, z, t + 1]))
-            cy[t] = c + y_next(c, cond[z, t + 1])
-        for t in range(1, TILES + 1):
-            u, c = q[0, z, t], cond[z, t]
-            wx[t] = 0.125 * (u + jnp.where(edge_high, u, x_next(u)))
-            cx[t] = c + jnp.where(edge_high, c, x_next(c))
-
-        def field(f, _):
-            spread = diff_ref[f]
-            vals = [q[f, z, t] for t in range(TILES + 2)]
-            diffs = [
-                y_next(vals[t], vals[min(t + 1, TILES + 1)]) - vals[t] for t in range(TILES + 2)
-            ]
-            halves = [
-                0.5 * minmod(y_back(diffs[t], diffs[max(t - 1, 0)]), diffs[t])
-                for t in range(TILES + 2)
-            ]
-            rights = [v - h for v, h in zip(vals, halves)]
-            nets = [
-                face(
-                    wy[t], cy[t], spread, diffs[t], vals[t] + halves[t],
-                    y_next(rights[t], rights[t + 1]),
-                )
-                for t in range(TILES + 1)
-            ]
-            for t in range(1, TILES + 1):
-                total = acc[f, z - 2, t - 1] + (nets[t] - y_back(nets[t], nets[t - 1]))
-                v = vals[t]
-                d = jnp.where(edge_high, 0.0, x_next(v) - v)
-                half = 0.5 * minmod(jnp.where(edge_low, 0.0, x_back(d)), d)
-                right = jnp.where(edge_high, v, x_next(v - half))
-                net = face(wx[t], cx[t], spread, d, v + half, right)
-                low = jnp.where(edge_low, -0.25 * q[0, z, t] * v, x_back(net))
-                total = total + (net - low)
-                start = pl.multiple_of((z - 2) * PLANE + (t - 1) * 128, 128)
-                out_ref[f, :, pl.ds(start, 128)] = total[:4]
-                out_ref[f, :, pl.ds(start + 16 * PLANE, 128)] = total[4:]
-            return 0
-
-        lax.fori_loop(0, F, field, 0)
-        return 0
-
-    lax.fori_loop(2, 18, along_yx, 0)
 
     def finish(k, _):
         move(0, k).wait_send()

time: 98.1 us -> 95.8 us (0.977)
  the two profiles are of different devices: /device:TPU:0 before, /device:TPU:17 now
where the time goes in v2:
time: 95.8 us; the launch traced here: 95.6 us
  Pallas kernels  91.8 us (96%)
  local copies, waits for them, and re-layouts  3.76 us (4%)
    pallas_call x1, Pallas kernels, local(): pl.pallas_call(body, out_shape=jax.ShapeDtypeStruct((F, CAP, cells), jnp....  91.8 us
    unnamed x1, local copies, waits for them, and re-layouts  3.76 us

profile of v2, /device:TPU:17, one launch (start us, length us, event | category | flops | bytes accessed | tf_op | source)
XLA Modules:
  0.0 95.6 jit_solution(8396214537007302845)
XLA Ops:
  0.0 91.8 %shard_map.37 = f32[6,4,32768]{2,1,0:T(4,128)} custom-call(s32[128]{0:T(128)} %refs_0_.1, f32[6]{0:T(128)} %refs_1_.1, f32[6,8,32768]{2,1,0:T(8,128)} %bitcast.3), custom_call_target="tpu_custom_call" | custom-call | tf_op jit(solution)/shard_map/pallas_call | solution.py:392
  91.8 3.8 %copy.5 = f32[4,6,32768]{2,0,1:T(4,128)} copy(f32[4,6,32768]{2,0,1:T(4,128)} %bitcast.2) | data formatting | bytes 6291456

commit v3 on v2

--- a/solution.py
+++ b/solution.py
@@ -16,7 +16,7 @@
 def kernel(
     n_gx, n_gy, owner_ref, diff_ref, state_ref, out_ref,
     held, send, recv, q, cond, acc, wz, cz, wy, cy, wx, cx,
-    zsend, zrecv, ysend, yrecv,
+    dy, dx, hy, hx, ny, nx, zsend, zrecv, ysend, yrecv,
     in_sem, move_send, move_recv, z_send, z_recv, y_send, y_recv,
 ):
     gx = lax.axis_index("gx")
@@ -67,6 +67,14 @@
     def turn(values, shift):
         return pltpu.roll(values, shift % 128, 1)
 
+    def each_field(work):
+        def group(g, _):
+            for f in range(F // 2):
+                work(g * (F // 2) + f)
+            return 0
+
+        lax.fori_loop(0, 2, group, 0)
+
     def tile_of(f, k, part, t):
         start = pl.multiple_of((k + 8 * part) * PLANE + t * 128, 128)
         return held[f, :, pl.ds(start, 128)]
@@ -85,7 +93,7 @@
         for part in range(4):
             in_copy(k, part).wait()
 
-        def field(f, _):
+        def field(f):
             for t in range(TILES):
                 a, b, c, d = (tile_of(f, k, part, t) for part in range(4))
                 a2, c6 = sub(a, 2), sub(c, 6)
@@ -97,9 +105,8 @@
                 )
                 send[0, k, f, t] = up
                 send[1, k, f, t] = down
-            return 0
-
-        lax.fori_loop(0, F, field, 0)
+
+        each_field(field)
         move(0, k).start()
         move(1, k).start()
         return 0
@@ -135,7 +142,7 @@
         move(0, k).wait_recv()
         move(1, k).wait_recv()
 
-        def field(f, _):
+        def field(f):
             for t in range(TILES):
                 a, b, c, d = (tile_of(f, k, part, t) for part in range(4))
                 up = recv[0, k, f, t]
@@ -156,9 +163,8 @@
                     ysend[1, k, f] = jnp.where(lane < 64, first, turn(second, 64))
                 if t == TILES - 1:
                     ysend[0, k, f] = jnp.where(lane < 64, turn(second, 64), first)
-            return 0
-
-        lax.fori_loop(0, F, field, 0)
+
+        each_field(field)
 
         @pl.when(gy < n_gy - 1)
         def _():
@@ -177,7 +183,7 @@
         def _():
             y_copy(1, k).wait_recv()
 
-        def field(f, _):
+        def field(f):
             lower = yrecv[0, k, f]
             upper = yrecv[1, k, f]
             for plane, low, high in (
@@ -191,9 +197,8 @@
                 q[f, plane, TILES + 1] = jnp.where(
                     gy == n_gy - 1, jnp.where(lane < 32, turn(top, 32), turn(top, 64)), high
                 )
-            return 0
-
-        lax.fori_loop(0, F, field, 0)
+
+        each_field(field)
 
     def conduct(z):
         for t in range(TILES + 2):
@@ -219,6 +224,23 @@
 
     def y_back(values, earlier):
         return turn(jnp.where(lane >= 96, earlier, values), 32)
+
+    def send_z():
+        def pack_z(f, _):
+            for t in range(1, TILES + 1):
+                zsend[1, f, t - 1] = jnp.where(row < 4, q[f, 2, t], sub(q[f, 3, t], 4))
+                zsend[0, f, t - 1] = jnp.where(row < 4, sub(q[f, 16, t], 4), q[f, 17, t])
+            return 0
+
+        lax.fori_loop(0, F, pack_z, 0)
+
+        @pl.when(gx < n_gx - 1)
+        def _():
+            z_copy(0).start()
+
+        @pl.when(gx > 0)
+        def _():
+            z_copy(1).start()
 
     def along_yx(z):
         conduct(z)
@@ -231,68 +253,74 @@
             wx[t] = 0.125 * (u + jnp.where(edge_high, u, x_next(u)))
             cx[t] = c + jnp.where(edge_high, c, x_next(c))
 
-        def field(f, _):
+        def differences(f):
+            vals = [q[f, z, t] for t in range(TILES + 2)]
+            for t in range(TILES + 2):
+                dy[f, t] = y_next(vals[t], vals[min(t + 1, TILES + 1)]) - vals[t]
+            for t in range(1, TILES + 1):
+                dx[f, t] = jnp.where(edge_high, 0.0, x_next(vals[t]) - vals[t])
+
+        def slopes(f):
+            diffs = [dy[f, t] for t in range(TILES + 2)]
+            for t in range(TILES + 2):
+                hy[f, t] = 0.5 * minmod(y_back(diffs[t], diffs[max(t - 1, 0)]), diffs[t])
+            for t in range(1, TILES + 1):
+                d = dx[f, t]
+                hx[f, t] = 0.5 * minmod(jnp.where(edge_low, 0.0, x_back(d)), d)
+
+        def fluxes(f):
             spread = diff_ref[f]
             vals = [q[f, z, t] for t in range(TILES + 2)]
-            diffs = [
-                y_next(vals[t], vals[min(t + 1, TILES + 1)]) - vals[t] for t in range(TILES + 2)
-            ]
-            halves = [
-                0.5 * minmod(y_back(diffs[t], diffs[max(t - 1, 0)]), diffs[t])
-                for t in range(TILES + 2)
-            ]
+            halves = [hy[f, t] for t in range(TILES + 2)]
             rights = [v - h for v, h in zip(vals, halves)]
-            nets = [
-                face(
-                    wy[t], cy[t], spread, diffs[t], vals[t] + halves[t],
+            for t in range(TILES + 1):
+                ny[f, t] = face(
+                    wy[t], cy[t], spread, dy[f, t], vals[t] + halves[t],
                     y_next(rights[t], rights[t + 1]),
                 )
-                for t in range(TILES + 1)
-            ]
             for t in range(1, TILES + 1):
-                total = vals[t] + (nets[t] - y_back(nets[t], nets[t - 1]))
-                v = vals[t]
-                d = jnp.where(edge_high, 0.0, x_next(v) - v)
-                half = 0.5 * minmod(jnp.where(edge_low, 0.0, x_back(d)), d)
+                v, half = vals[t], hx[f, t]
                 right = jnp.where(edge_high, v, x_next(v - half))
-                net = face(wx[t], cx[t], spread, d, v + half, right)
+                nx[f, t] = face(wx[t], cx[t], spread, dx[f, t], v + half, right)
+
+        def sums(f):
+            nets = [ny[f, t] for t in range(TILES + 1)]
+            for t in range(1, TILES + 1):
+                v, net = q[f, z, t], nx[f, t]
+                total = v + (nets[t] - y_back(nets[t], nets[t - 1]))
                 low = jnp.where(edge_low, -0.25 * q[0, z, t] * v, x_back(net))
-                total = total + (net - low)
-                acc[f, z - 2, t - 1] = total
-            return 0
-
-        lax.fori_loop(0, F, field, 0)
+                acc[f, z - 2, t - 1] = total + (net - low)
+
+        each_field(differences)
+        each_field(slopes)
+        each_field(fluxes)
+        each_field(sums)
 
     def update(k):
         fill_y(k)
-        along_yx(k + 2)
-        along_yx(k + 10)
+
+        def plane(i, _):
+            along_yx(k + 2 + 8 * i)
+            return 0
+
+        lax.fori_loop(0, 2, plane, 0)
 
     def step(k, _):
-        gather(k)
-        update(k - 1)
-        return 0
-
-    gather(0)
-    lax.fori_loop(1, CHUNKS, step, 0)
-
-    def pack_z(f, _):
-        for t in range(1, TILES + 1):
-            zsend[1, f, t - 1] = jnp.where(row < 4, q[f, 2, t], sub(q[f, 3, t], 4))
-            zsend[0, f, t - 1] = jnp.where(row < 4, sub(q[f, 16, t], 4), q[f, 17, t])
-        return 0
-
-    lax.fori_loop(0, F, pack_z, 0)
-
-    @pl.when(gx < n_gx - 1)
-    def _():
-        z_copy(0).start()
-
-    @pl.when(gx > 0)
-    def _():
-        z_copy(1).start()
-
-    update(CHUNKS - 1)
+        @pl.when(k < CHUNKS)
+        def _():
+            gather(k)
+
+        @pl.when(k == CHUNKS)
+        def _():
+            send_z()
+
+        @pl.when(k > 0)
+        def _():
+            update(k - 1)
+
+        return 0
+
+    lax.fori_loop(0, CHUNKS + 1, step, 0)
 
     @pl.when(gx > 0)
     def _():
@@ -411,6 +439,7 @@
                 vmem((TILES + 2, 8, 128), jnp.float32),
                 vmem((TILES + 2, 8, 128), jnp.float32),
                 vmem((TILES + 2, 8, 128), jnp.float32),
+                *[vmem((F, TILES + 2, 8, 128), jnp.float32) for _ in range(6)],
                 vmem((2, F, TILES, 8, 128), jnp.float32),
                 vmem((2, F, TILES, 8, 128), jnp.float32),
                 vmem((2, CHUNKS, F, 8, 128), jnp.float32),

time: 95.8 us -> 81.4 us (0.85)
  the two profiles are of different devices: /device:TPU:17 before, /device:TPU:0 now
where the time goes in v3:
time: 81.4 us; the launch traced here: 79.8 us
  Pallas kernels  76.1 us (93%)
  local copies, waits for them, and re-layouts  3.76 us (5%)
    pallas_call x1, Pallas kernels, local(): pl.pallas_call(body, out_shape=jax.ShapeDtypeStruct((F, CAP, cells), jnp....  76.1 us
    unnamed x1, local copies, waits for them, and re-layouts  3.76 us

profile of v3, /device:TPU:0, one launch (start us, length us, event | category | flops | bytes accessed | tf_op | source)
XLA Modules:
  0.0 79.8 jit_solution(2750875605047367696)
XLA Ops:
  0.0 76.1 %shard_map.37 = f32[6,4,32768]{2,1,0:T(4,128)} custom-call(s32[128]{0:T(128)} %refs_0_.1, f32[6]{0:T(128)} %refs_1_.1, f32[6,8,32768]{2,1,0:T(8,128)} %bitcast.3), custom_call_target="tpu_custom_call" | custom-call | tf_op jit(solution)/shard_map/pallas_call | solution.py:420
  76.1 3.8 %copy.5 = f32[4,6,32768]{2,0,1:T(4,128)} copy(f32[4,6,32768]{2,0,1:T(4,128)} %bitcast.2) | data formatting | bytes 6291456

commit v4 on v3

--- a/solution.py
+++ b/solution.py
@@ -7,6 +7,7 @@
 
 F = 6
 CAP = 4
+AHEAD = 2
 CHUNKS = 8
 TILES = 8
 PLANE = 1024
@@ -89,6 +90,10 @@
             device_id_type=MESH,
         )
 
+    def start_move(k):
+        move(0, k).start()
+        move(1, k).start()
+
     def pack(k, _):
         for part in range(4):
             in_copy(k, part).wait()
@@ -107,8 +112,10 @@
                 send[1, k, f, t] = down
 
         each_field(field)
-        move(0, k).start()
-        move(1, k).start()
+        @pl.when(k < AHEAD)
+        def _():
+            start_move(k)
+
         return 0
 
     lax.fori_loop(0, CHUNKS, pack, 0)
@@ -141,6 +148,10 @@
     def gather(k):
         move(0, k).wait_recv()
         move(1, k).wait_recv()
+
+        @pl.when(k < CHUNKS - AHEAD)
+        def _():
+            start_move(k + AHEAD)
 
         def field(f):
             for t in range(TILES):
@@ -314,13 +325,13 @@
         def _():
             send_z()
 
-        @pl.when(k > 0)
-        def _():
-            update(k - 1)
-
-        return 0
-
-    lax.fori_loop(0, CHUNKS + 1, step, 0)
+        @pl.when(k >= AHEAD)
+        def _():
+            update(k - AHEAD)
+
+        return 0
+
+    lax.fori_loop(0, CHUNKS + AHEAD, step, 0)
 
     @pl.when(gx > 0)
     def _():

time: 81.4 us -> 66 us (0.81); the launches traced: 79.8 us -> 65.8 us
  Pallas kernels: 76.1 us -> 62.1 us
    pallas_call x1, Pallas kernels: 76.1 us -> 62.1 us  [local(): pl.pallas_call(body, out_shape=jax.ShapeDtypeStruct((F, CAP, cells), jnp....]
where the time goes in v4:
time: 66 us; the launch traced here: 65.8 us
  Pallas kernels  62.1 us (94%)
  local copies, waits for them, and re-layouts  3.76 us (6%)
    pallas_call x1, Pallas kernels, local(): pl.pallas_call(body, out_shape=jax.ShapeDtypeStruct((F, CAP, cells), jnp....  62.1 us
    unnamed x1, local copies, waits for them, and re-layouts  3.76 us

profile of v4, /device:TPU:0, one launch (start us, length us, event | category | flops | bytes accessed | tf_op | source)
XLA Modules:
  0.0 65.8 jit_solution(17461786371956674537)
XLA Ops:
  0.0 62.1 %shard_map.37 = f32[6,4,32768]{2,1,0:T(4,128)} custom-call(s32[128]{0:T(128)} %refs_0_.1, f32[6]{0:T(128)} %refs_1_.1, f32[6,8,32768]{2,1,0:T(8,128)} %bitcast.3), custom_call_target="tpu_custom_call" | custom-call | tf_op jit(solution)/shard_map/pallas_call | solution.py:431
  62.1 3.8 %copy.5 = f32[4,6,32768]{2,0,1:T(4,128)} copy(f32[4,6,32768]{2,0,1:T(4,128)} %bitcast.2) | data formatting | bytes 6291456

commit v5 on v4

--- a/solution.py
+++ b/solution.py
@@ -302,10 +302,14 @@
                 low = jnp.where(edge_low, -0.25 * q[0, z, t] * v, x_back(net))
                 acc[f, z - 2, t - 1] = total + (net - low)
 
-        each_field(differences)
-        each_field(slopes)
-        each_field(fluxes)
-        each_field(sums)
+        for f in range(F):
+            differences(f)
+        for f in range(F):
+            slopes(f)
+        for f in range(F):
+            fluxes(f)
+        for f in range(F):
+            sums(f)
 
     def update(k):
         fill_y(k)
@@ -364,7 +368,7 @@
             wz[i] = 0.125 * (q[2, i + 1, t] + q[2, i + 2, t])
             cz[i] = cond[i + 1, t] + cond[i + 2, t]
 
-        def field(f, _):
+        def field(f):
             spread = diff_ref[f]
             here = q[f, 1, t]
             d_low = here - q[f, 0, t]
@@ -386,9 +390,8 @@
                     out_ref[f, :, pl.ds(start, 128)] = total[:4]
                     out_ref[f, :, pl.ds(start + 16 * PLANE, 128)] = total[4:]
                 before = net
-            return 0
-
-        lax.fori_loop(0, F, field, 0)
+
+        each_field(field)
         return 0
 
     lax.fori_loop(1, TILES + 1, along_z, 0)

time: 66 us -> 64.1 us (0.971)
  Pallas kernels: 62.1 us -> 60.1 us
    pallas_call x1, Pallas kernels: 62.1 us -> 60.1 us  [local(): pl.pallas_call(body, out_shape=jax.ShapeDtypeStruct((F, CAP, cells), jnp....]
where the time goes in v5:
time: 64.1 us; the launch traced here: 63.9 us
  Pallas kernels  60.1 us (94%)
  local copies, waits for them, and re-layouts  3.76 us (6%)
    pallas_call x1, Pallas kernels, local(): pl.pallas_call(body, out_shape=jax.ShapeDtypeStruct((F, CAP, cells), jnp....  60.1 us
    unnamed x1, local copies, waits for them, and re-layouts  3.76 us

profile of v5, /device:TPU:0, one launch (start us, length us, event | category | flops | bytes accessed | tf_op | source)
XLA Modules:
  0.0 63.9 jit_solution(14336511826566799669)
XLA Ops:
  0.0 60.1 %shard_map.37 = f32[6,4,32768]{2,1,0:T(4,128)} custom-call(s32[128]{0:T(128)} %refs_0_.1, f32[6]{0:T(128)} %refs_1_.1, f32[6,8,32768]{2,1,0:T(8,128)} %bitcast.3), custom_call_target="tpu_custom_call" | custom-call | tf_op jit(solution)/shard_map/pallas_call | solution.py:434
  60.1 3.8 %copy.5 = f32[4,6,32768]{2,0,1:T(4,128)} copy(f32[4,6,32768]{2,0,1:T(4,128)} %bitcast.2) | data formatting | bytes 6291456

commit v6 on v5

--- a/solution.py
+++ b/solution.py
@@ -7,7 +7,8 @@
 
 F = 6
 CAP = 4
-AHEAD = 2
+AHEAD = 3
+LAG = 2
 CHUNKS = 8
 TILES = 8
 PLANE = 1024
@@ -149,10 +150,6 @@
         move(0, k).wait_recv()
         move(1, k).wait_recv()
 
-        @pl.when(k < CHUNKS - AHEAD)
-        def _():
-            start_move(k + AHEAD)
-
         def field(f):
             for t in range(TILES):
                 a, b, c, d = (tile_of(f, k, part, t) for part in range(4))
@@ -184,6 +181,10 @@
         @pl.when(gy > 0)
         def _():
             y_copy(1, k).start()
+
+        @pl.when(k < CHUNKS - AHEAD)
+        def _():
+            start_move(k + AHEAD)
 
     def fill_y(k):
         @pl.when(gy > 0)
@@ -329,13 +330,13 @@
         def _():
             send_z()
 
-        @pl.when(k >= AHEAD)
-        def _():
-            update(k - AHEAD)
-
-        return 0
-
-    lax.fori_loop(0, CHUNKS + AHEAD, step, 0)
+        @pl.when(k >= LAG)
+        def _():
+            update(k - LAG)
+
+        return 0
+
+    lax.fori_loop(0, CHUNKS + LAG, step, 0)
 
     @pl.when(gx > 0)
     def _():
@@ -467,7 +468,7 @@
                 dma((2, CHUNKS)),
             ],
             compiler_params=pltpu.CompilerParams(
-                collective_id=0, has_side_effects=True, vmem_limit_bytes=56 * 2**20
+                collective_id=0, has_side_effects=True, vmem_limit_bytes=50 * 2**20
             ),
         )(old_owner, diffusivity, jnp.transpose(old_state, (1, 0, 2)))
         return jnp.transpose(result, (1, 0, 2))

time: 64.1 us -> 60.6 us (0.945)
  Pallas kernels: 60.1 us -> 57.5 us
  local copies, waits for them, and re-layouts: 3.76 us -> 2.98 us
    pallas_call x1, Pallas kernels: 60.1 us -> 57.5 us  [local(): pl.pallas_call(body, out_shape=jax.ShapeDtypeStruct((F, CAP, cells), jnp....]
    unnamed x1 -> x5, local copies, waits for them, and re-layouts: 3.76 us -> 2.98 us
where the time goes in v6:
time: 60.6 us; the launch traced here: 60.4 us
  Pallas kernels  57.5 us (95%)
  local copies, waits for them, and re-layouts  2.98 us (5%)
    pallas_call x1, Pallas kernels, local(): pl.pallas_call(body, out_shape=jax.ShapeDtypeStruct((F, CAP, cells), jnp....  57.5 us
    unnamed x5, local copies, waits for them, and re-layouts  2.98 us

profile of v6, /device:TPU:0, one launch (start us, length us, event | category | flops | bytes accessed | tf_op | source)
XLA Modules:
  0.0 60.4 jit_solution(17571988970106868634)
XLA Ops:
  0.0 0.0 copy-start
  0.0 0.7 %copy-done = s32[128]{0:T(128)S(1)} copy-done((s32[128]{0:T(128)S(1)}, s32[128]{0:T(128)}, u32[]{:S(2)}) %copy-start) | copy-done | bytes 536
  0.7 0.0 copy-start.1
  0.7 0.7 %copy-done.1 = f32[6]{0:T(128)S(1)} copy-done((f32[6]{0:T(128)S(1)}, f32[6]{0:T(128)}, u32[]{:S(2)}) %copy-start.1) | copy-done | bytes 48
  1.3 57.5 %shard_map.37 = f32[6,4,32768]{2,1,0:T(4,128)S(1)} custom-call(s32[128]{0:T(128)S(1)} %copy-done, f32[6]{0:T(128)S(1)} %copy-done.1, f32[6,8,32768]{2,1,0:T(8,128)} %bitcast.3), custom_call_target="tpu_custom_call" | custom-call | tf_op jit(solution)/shard_map/pallas_call | solution.py:435
  58.8 1.7 %copy.5 = f32[4,6,32768]{2,0,1:T(4,128)} copy(f32[4,6,32768]{2,0,1:T(4,128)S(1)} %bitcast.2) | data formatting | bytes 6291456
Async XLA Ops:
  0.0 0.7 %copy-start = (s32[128]{0:T(128)S(1)}, s32[128]{0:T(128)}, u32[]{:S(2)}) copy-start(s32[128]{0:T(128)} %refs_0_.1) | copy-start | bytes 1540
  0.7 0.7 %copy-start.1 = (f32[6]{0:T(128)S(1)}, f32[6]{0:T(128)}, u32[]{:S(2)}) copy-start(f32[6]{0:T(128)} %refs_1_.1) | copy-start | bytes 76
